TPU v7x, 256 devices: a whole 4x4x8 slice. The times are simulated.
256 devices in a mesh: ed: 16 (over z, core), ep: 16 (over x, y).
Axes of the slice: x: 4, y: 4, z: 8, core: 2. Of those that a mesh axis runs over, the one named last changes fastest.
Arguments:
- grad_out: bfloat16 [14336, 4096], P(('ed', 'ep')), may hold values from -6 to 6
- routes: int32 [14336, 8], P(('ed', 'ep')), may hold values from 0 to 15, all different within a row; in each aligned block of 56 rows (0 to 55, 56 to 111, ...) at most 35 rows name the same one
- gates: bfloat16 [14336, 8], P(('ed', 'ep')), may hold values from 0.049804688 to 0.29882812
- hidden: bfloat16 [16, 16, 16, 35, 1536], P('ed', None, 'ep'), may hold values from -0.29882812 to 0.29882812
- master: float32 [16, 4096, 1536], P('ep', 'ed'), may hold values from -0.15625 to 0.15625
- moment_one: float32 [16, 4096, 1536], P('ep', 'ed'), may hold values from -3 to 3
- moment_two: float32 [16, 4096, 1536], P('ep', 'ed'), may hold values from 0.02 to 1
Outputs:
- grad_gates: float32 [14336, 8], P(('ed', 'ep'))
- grad_hidden: bfloat16 [16, 16, 16, 35, 1536], P('ed', None, 'ep')
- new_master: float32 [16, 4096, 1536], P('ep', 'ed')
- new_moment_one: float32 [16, 4096, 1536], P('ep', 'ed')
- new_moment_two: float32 [16, 4096, 1536], P('ep', 'ed')
Inputs may be any that keep to these rules, and one draw needn't show every extreme that they name: `routes`: each row names 8 different experts; among the 56 rows of one device no expert is named by more than 35 rows, a bound that some block reaches.
All inputs are finite; a program needn't handle non-finite values.
Results may differ from a plain program's by a relative error of at most 0.008.
Values may be sent and summed in bfloat16 or wider, within the bound.
A program may use at most 192 MiB of HBM per device.

v0:
```python
import jax
import jax.numpy as jnp
from jax import lax
from jax.sharding import PartitionSpec as P

beta_first = 0.9
beta_second = 0.95
learn_rate = 0.01
adam_eps = 1e-08


def local(grad_out, routes, gates, hidden, master, moment_one, moment_two):
    experts = lax.axis_size("ep")
    tokens_here = grad_out.shape[0]
    model_width = grad_out.shape[1]
    top_count = routes.shape[1]
    capacity = hidden.shape[3]
    hidden_width = hidden.shape[4]
    row_count = experts * capacity
    flat_routes = routes.reshape(-1)
    onehot = (flat_routes[:, None] == jnp.arange(experts, dtype=jnp.int32)[None, :]).astype(
        jnp.int32
    )
    before = jnp.cumsum(onehot, axis=0) - onehot
    slot_index = jnp.sum(before * onehot, axis=1)
    target = flat_routes * capacity + slot_index
    places = jnp.arange(row_count, dtype=jnp.int32)
    matches = target[None, :] == places[:, None]
    token_pick = jnp.sum(
        matches.reshape(row_count, tokens_here, top_count).astype(jnp.int32), axis=2
    ).astype(jnp.bfloat16)
    send_rows = jnp.dot(token_pick, grad_out, preferred_element_type=jnp.float32).astype(
        jnp.bfloat16
    )
    gate_values = gates.reshape(-1).astype(jnp.float32)
    send_gates = jnp.sum(jnp.where(matches, gate_values[None, :], 0.0), axis=1).astype(jnp.bfloat16)
    rows_in, gates_in = (
        lax.all_to_all(
            send_rows.reshape(experts, 1, capacity, model_width),
            "ep",
            split_axis=0,
            concat_axis=0,
            tiled=True,
        ),
        lax.all_to_all(
            send_gates.reshape(experts, 1, capacity), "ep", split_axis=0, concat_axis=0, tiled=True
        ),
    )
    grad_rows = rows_in.reshape(row_count, model_width)
    gate_rows = gates_in.reshape(row_count, 1).astype(jnp.float32)
    saved_rows = hidden.reshape(row_count, hidden_width)
    weights = master.astype(jnp.bfloat16)
    block = lax.all_gather(weights, "ed", axis=1, tiled=True)[0]
    upward = jnp.dot(grad_rows, block, preferred_element_type=jnp.float32)
    prob_slot = jnp.sum(upward * saved_rows.astype(jnp.float32), axis=1)
    prob_back = lax.all_to_all(
        prob_slot.reshape(experts, 1, capacity), "ep", split_axis=0, concat_axis=0, tiled=True
    )
    grad_gates = jnp.take(prob_back.reshape(row_count), target).reshape(tokens_here, top_count)
    grad_hidden = (gate_rows * upward).astype(jnp.bfloat16).reshape(hidden.shape)
    weighted = (gate_rows * grad_rows.astype(jnp.float32)).astype(jnp.bfloat16)
    gradient = lax.psum_scatter(
        lax.dot_general(
            weighted, saved_rows, (((0,), (0,)), ((), ())), preferred_element_type=jnp.float32
        ).astype(jnp.bfloat16),
        "ed",
        scatter_dimension=0,
        tiled=True,
    ).astype(jnp.float32)
    gradient = gradient.reshape(master.shape)
    new_moment_one = beta_first * moment_one + (1.0 - beta_first) * gradient
    new_moment_two = beta_second * moment_two + (1.0 - beta_second) * gradient * gradient
    first_bias = 1.0 - beta_first**20
    second_bias = 1.0 - beta_second**20
    update = new_moment_one / first_bias / (jnp.sqrt(new_moment_two / second_bias) + adam_eps)
    new_master = master - learn_rate * update
    return (grad_gates, grad_hidden, new_master, new_moment_one, new_moment_two)


def solution(mesh):
    in_specs = (
        P(("ed", "ep"), None),
        P(("ed", "ep"), None),
        P(("ed", "ep"), None),
        P("ed", None, "ep", None, None),
        P("ep", "ed", None),
        P("ep", "ed", None),
        P("ep", "ed", None),
    )
    out_specs = (
        P(("ed", "ep"), None),
        P("ed", None, "ep", None, None),
        P("ep", "ed", None),
        P("ep", "ed", None),
        P("ep", "ed", None),
    )
    return jax.shard_map(local, mesh=mesh, in_specs=in_specs, out_specs=out_specs, check_vma=False)
```

profile of v0, /device:TPU:1, one launch (start us, length us, event | category | flops | bytes accessed | tf_op | source)
XLA Modules:
  0.0 345.0 jit_solution(7067409950417047045)
XLA Ops:
  7.2 0.8 copy.42
  8.1 1.2 reduce-window.6
  9.7 0.8 copy.48
  10.7 0.7 convert_element_type.101
  11.4 7.6 %all-to-all-start.2 = ((bf16[16,1,35]{2,1,0:T(2,128)(2,1)}), bf16[16,1,35]{2,1,0:T(2,128)(2,1)S(1)}, u32[]{:S(2)}, u32[]{:S(2)}) async-start(bf16[16,1,35]{2,1,0:T(2,128)(2,1)} %convert_element_type.101), calls=%async_computation.2 | async-start | bytes 16384 | tf_op jit(solution)/shard_map/all_to_all | solution.py:45
  19.6 3.5 %convolution_convert_fusion.1 = bf16[560,4096]{1,0:T(8,128)(2,1)} fusion(bf16[56,4096]{1,0:T(8,128)(2,1)S(1)} %copy-done, s32[560,56]{0,1:T(8,128)S(1)} %convert_reduce_fusion), kind=kOutput, calls=%fused_computation.5 | convolution fusion | flops 259226240 | bytes 5171712 | tf_op jit(solution)/shard_map/dot_general | solution.py:32
  23.1 4.7 %reshape.144 = bf16[16,1,35,4096]{3,2,0,1:T(8,128)(2,1)} reshape(bf16[560,4096]{1,0:T(8,128)(2,1)} %convolution_convert_fusion.1) | data formatting | bytes 9175040 | tf_op jit(solution)/shard_map/reshape | solution.py:39
  27.8 6.7 %all-to-all-start = ((bf16[16,1,35,4096]{3,2,1,0:T(8,128)(2,1)}), bf16[16,1,35,4096]{3,2,1,0:T(8,128)(2,1)}, u32[]{:S(2)}, u32[]{:S(2)}) async-start(bf16[16,1,35,4096]{3,2,1,0:T(8,128)(2,1)} %bitcast.37), calls=%async_computation | async-start | bytes 10485760 | tf_op jit(solution)/shard_map/all_to_all | solution.py:38
  34.5 2.4 copy.47
  37.0 1.5 reshape.146
  38.5 74.3 %all-to-all-done = bf16[16,1,35,4096]{3,2,1,0:T(8,128)(2,1)} async-done(((bf16[16,1,35,4096]{3,2,1,0:T(8,128)(2,1)}), bf16[16,1,35,4096]{3,2,1,0:T(8,128)(2,1)}, u32[]{:S(2)}, u32[]{:S(2)}) %all-to-all-start) | async-done | bytes 4587552 | tf_op jit(solution)/shard_map/all_to_all | solution.py:38
  112.7 6.8 %multiply_convert_fusion = bf16[16,1,35,4096]{3,2,1,0:T(8,128)(2,1)} fusion(bf16[16,1,35,4096]{3,2,1,0:T(8,128)(2,1)} %all-to-all-done, f32[16,35]{1,0:T(8,128)S(1)} %bitcast.39), kind=kLoop, calls=%fused_computation.4 | loop fusion | flops 6881280 | bytes 9177280 | tf_op jit(solution)/shard_map/convert_element_type | solution.py:61
  119.6 4.8 %convert_element_type.95 = bf16[560,4096]{1,0:T(8,128)(2,1)} reshape(bf16[16,1,35,4096]{3,2,1,0:T(8,128)(2,1)} %multiply_convert_fusion) | data formatting | bytes 9175040 | tf_op jit(solution)/shard_map/convert_element_type | solution.py:61
  124.4 14.8 %convolution_convert_fusion = bf16[4096,1536]{1,0:T(8,128)(2,1)} fusion(bf16[560,4096]{1,0:T(8,128)(2,1)} %convert_element_type.95, bf16[560,1536]{1,0:T(8,128)(2,1)S(1)} %copy-done.2), kind=kOutput, calls=%fused_computation.1 | convolution fusion | flops 7052722176 | bytes 18890752 | tf_op jit(solution)/shard_map/dot_general | solution.py:63
  139.5 85.1 %reduce-scatter.2.cloned.1.call-done = bf16[256,1536]{1,0:T(8,128)(2,1)} async-done(((bf16[4096,1536]{1,0:T(8,128)(2,1)}), bf16[256,1536]{1,0:T(8,128)(2,1)}) %reduce-scatter.2.cloned.1.call-update) | async-done | bytes 786448 | tf_op jit(solution)/shard_map/reduce_scatter | solution.py:62
  224.6 6.2 %multiply_subtract_fusion = (f32[1,256,1536]{2,1,0:T(8,128)}, f32[1,256,1536]{2,1,0:T(8,128)}, f32[1,256,1536]{2,1,0:T(8,128)}, bf16[1,256,1536]{2,1,0:T(8,128)(2,1)}) fusion(f32[1,256,1536]{2,1,0:T(8,128)} %param.11, bf16[256,1536]{1,0:T(8,128)(2,1)} %reduce-scatter.2.cloned.1.call-done, f32[1,256,1536]{2,1,0:T(8,128)} %param.12, f32[1,256,1536]{2,1,0:T(8,128)} %param.13), kind=kLoop, calls=%fused_computation.14 | loop fusion | flops 5898240 | bytes 11010048 | tf_op jit(solution)/shard_map/sub | solution.py:76
  231.1 4.7 %reshape.145 = bf16[560,4096]{1,0:T(8,128)(2,1)} reshape(bf16[16,1,35,4096]{3,2,1,0:T(8,128)(2,1)} %all-to-all-done) | data formatting | bytes 9175040 | tf_op jit(solution)/shard_map/reshape | solution.py:49
  235.8 71.9 %all-gather.2.cloned.1.call-done = bf16[1,4096,1536]{2,1,0:T(8,128)(2,1)} async-done(((bf16[1,256,1536]{2,1,0:T(8,128)(2,1)}), bf16[1,4096,1536]{2,1,0:T(8,128)(2,1)}) %all-gather.2.cloned.1.call-update) | async-done | bytes 12582928 | tf_op jit(solution)/shard_map/all_gather | solution.py:53
  307.7 12.7 %multiply_convert_fusion.1 = (bf16[560,1536]{1,0:T(8,128)(2,1)}, f32[560]{0:T(1024)S(1)}) fusion(f32[560]{0:T(1024)S(1)} %reshape.152, bf16[560,1536]{1,0:T(8,128)(2,1)S(1)} %copy-done.2, bf16[560,4096]{1,0:T(8,128)(2,1)} %reshape.145, bf16[1,4096,1536]{2,1,0:T(8,128)(2,1)} %all-gather.2.cloned.1.call-done), kind=kOutput, calls=%fused_computation.6 | convolution fusion | flops 7050731008 | bytes 20615552 | tf_op jit(solution)/shard_map/dot_general | solution.py:54
  321.1 6.5 %all-to-all-start.1 = ((f32[16,1,35]{2,1,0:T(1,128)}), f32[16,1,35]{2,1,0:T(1,128)S(1)}, u32[]{:S(2)}, u32[]{:S(2)}) async-start(f32[16,1,35]{2,1,0:T(1,128)} %reshape.147), calls=%async_computation.1 | async-start | bytes 16384 | tf_op jit(solution)/shard_map/all_to_all | solution.py:56
  327.6 1.7 reshape.149
  329.4 1.7 copy.51
  331.1 2.9 all-to-all-done.1
  335.3 2.1 gather_fusion
  (38 shorter events, 4.5 us)
Async XLA Ops:
  7.2 12.4 %copy-start = (bf16[56,4096]{1,0:T(8,128)(2,1)S(1)}, bf16[56,4096]{1,0:T(8,128)(2,1)}, u32[]{:S(2)}) copy-start(bf16[56,4096]{1,0:T(8,128)(2,1)} %param.7) | copy-start | bytes 1376260
  11.4 16.3 %all-to-all-start.2 = ((bf16[16,1,35]{2,1,0:T(2,128)(2,1)}), bf16[16,1,35]{2,1,0:T(2,128)(2,1)S(1)}, u32[]{:S(2)}, u32[]{:S(2)}) async-start(bf16[16,1,35]{2,1,0:T(2,128)(2,1)} %convert_element_type.101), calls=%async_computation.2 | async-start | bytes 16384 | tf_op jit(solution)/shard_map/all_to_all | solution.py:45
  27.8 85.0 %all-to-all-start = ((bf16[16,1,35,4096]{3,2,1,0:T(8,128)(2,1)}), bf16[16,1,35,4096]{3,2,1,0:T(8,128)(2,1)}, u32[]{:S(2)}, u32[]{:S(2)}) async-start(bf16[16,1,35,4096]{3,2,1,0:T(8,128)(2,1)} %bitcast.37), calls=%async_computation | async-start | bytes 10485760 | tf_op jit(solution)/shard_map/all_to_all | solution.py:38
  34.5 190.1 %reduce-scatter.2.cloned.1.call-start = ((), (), s32[]{:S(2)}) async-start(), calls=%async_computation.5 | async-start | bytes 13369344 | tf_op jit(solution)/shard_map/reduce_scatter | solution.py:62
  119.6 4.8 %copy-start.2 = (bf16[560,1536]{1,0:T(8,128)(2,1)S(1)}, bf16[560,1536]{1,0:T(8,128)(2,1)}, u32[]{:S(2)}) copy-start(bf16[560,1536]{1,0:T(8,128)(2,1)} %reshape.146) | copy-start | bytes 5160964
  139.3 168.4 %all-gather.2.cloned.1.call-start = ((), (), s32[]{:S(2)}) async-start(), calls=%async_computation.4 | async-start | bytes 13369344 | tf_op jit(solution)/shard_map/all_gather | solution.py:53
  321.1 12.9 %all-to-all-start.1 = ((f32[16,1,35]{2,1,0:T(1,128)}), f32[16,1,35]{2,1,0:T(1,128)S(1)}, u32[]{:S(2)}, u32[]{:S(2)}) async-start(f32[16,1,35]{2,1,0:T(1,128)} %reshape.147), calls=%async_computation.1 | async-start | bytes 16384 | tf_op jit(solution)/shard_map/all_to_all | solution.py:56
  329.4 8.8 %copy-start.1 = (bf16[56,4096]{1,0:T(8,128)(2,1)S(1)}, bf16[56,4096]{1,0:T(8,128)(2,1)}, u32[]{:S(2)}) copy-start(bf16[56,4096]{1,0:T(8,128)(2,1)} %param.7) | copy-start | bytes 1376260
Sparse Core Ops, SparseCore 0:
  139.4 85.1 reduce-scatter.1
  231.0 76.6 all-gather.1
where the time goes:
time: 345 us
  waiting for transfers between devices  234 us (68%)
  matrix products  31 us (9%)
  local copies, waits for them, and re-layouts  28.7 us (8%)
  starting transfers between devices  21.1 us (6%)
  other arithmetic  15.8 us (5%)
  between operations  14.2 us (4%)
    reduce_scatter x1, waiting for transfers between devices, local(): lax.psum_scatter(lax.dot_general(weighted, saved_rows, (((0,), (0,)), (()...  85.1 us
    all_to_all x1, waiting for transfers between devices, local(): lax.all_to_all(send_rows.reshape(experts, 1, capacity, model_width), 'ep'...  74.3 us
    all_gather x1, waiting for transfers between devices, local(): block = lax.all_gather(weights, 'ed', axis=1, tiled=True)[0]  71.9 us
    dot_general x1, matrix products, local(): lax.dot_general(weighted, saved_rows, (((0,), (0,)), ((), ())), preferred...  14.8 us
    dot_general x1, matrix products, local(): upward = jnp.dot(grad_rows, block, preferred_element_type=jnp.float32)  12.7 us
    all_to_all x1, starting transfers between devices, local(): lax.all_to_all(send_gates.reshape(experts, 1, capacity), 'ep', split_axis...  7.58 us
  transfers between devices with their start and end apart: 5, of which 4 were waited for; matrix products, arithmetic and copies ran while one was open for 6% of the time, Pallas kernels for 0%

commit v1 on v0

v1 whole, which is shorter than its diff:
```python
import jax
import jax.numpy as jnp
from jax import lax
from jax.experimental import pallas as pl
from jax.experimental.pallas import tpu as pltpu
from jax.sharding import PartitionSpec as P

beta_first = 0.9
beta_second = 0.95
learn_rate = 0.01
adam_eps = 1e-08

MESH = pl.DeviceIdType.MESH
BF = jnp.bfloat16
F32 = jnp.float32
I32 = jnp.int32

NZ = 8
SIDE = 4
EXP = 16
TOK = 56
ROWS = 64
ALL = EXP * ROWS
WIDTH = 4096
HID = 1536
HALF = HID // 2
CAP = 35
SLOTS = CAP * EXP
OWN = 256
COL = 256


def dot(a, b):
    return jnp.dot(a, b, preferred_element_type=F32)


def body(
    go_ref, routes_ref, gates_ref, hid_ref, master_ref,
    gh_ref, grad_ref, gg_ref,
    tok, wts, gd, tile, gatec, sel_t, h_tok, hg_t, acc, gmul, pown, stage, psib, rsb, prob, probr,
    xy_s, xy_r, zw_s, zw_r, sw_s, sw_r, gd_s, gd_r, ps_s, ps_r, rs_s, rs_r, pr_s, pr_r,
):
    ed = lax.axis_index("ed")
    ep = lax.axis_index("ep")
    z, c = ed // 2, ed % 2
    x, y = ep // SIDE, ep % SIDE

    def zdev(k):
        return {"ed": lax.rem(z + k + NZ, NZ) * 2 + c, "ep": ep}

    sibling = {"ed": z * 2 + 1 - c, "ep": ep}

    def peer(o):
        return lax.rem(ep + o, EXP)

    def send(src, dst, ssem, rsem, dev):
        copy = pltpu.make_async_remote_copy(
            src_ref=src, dst_ref=dst, send_sem=ssem, recv_sem=rsem,
            device_id=dev, device_id_type=MESH,
        )
        copy.start()

    def arrived(ref, rsem, ssem):
        pltpu.make_async_remote_copy(
            src_ref=ref, dst_ref=ref, send_sem=ssem, recv_sem=rsem,
            device_id=sibling, device_id_type=MESH,
        ).wait_recv()

    def sent(ref, ssem, rsem):
        pltpu.make_async_remote_copy(
            src_ref=ref, dst_ref=ref, send_sem=ssem, recv_sem=rsem,
            device_id=sibling, device_id_type=MESH,
        ).wait_send()

    barrier = pltpu.get_barrier_semaphore()

    def greet(o, carry):
        pl.semaphore_signal(barrier, inc=1, device_id={"ed": ed, "ep": peer(o)}, device_id_type=MESH)
        return carry

    lax.fori_loop(1, EXP, greet, 0)
    for dev in (zdev(1), zdev(-1), sibling):
        pl.semaphore_signal(barrier, inc=1, device_id=dev, device_id_type=MESH)

    wts[ed] = master_ref[...].astype(BF)
    for q in range(4):
        cols = pl.ds(q * 1024, 1024)
        wide = go_ref[:, cols].astype(F32)
        tok[ep, :, cols] = jnp.concatenate([wide, jnp.zeros((ROWS - TOK, 1024), F32)], axis=0).astype(BF)
    expert_row = lax.broadcasted_iota(I32, (EXP, TOK), 0)
    dense = jnp.zeros((EXP, TOK), F32)
    named = jnp.zeros((EXP, TOK), F32)
    for k in range(routes_ref.shape[0]):
        hit = routes_ref[k : k + 1, :] == expert_row
        dense = dense + jnp.where(hit, gates_ref[k : k + 1, :].astype(F32), 0.0)
        named = named + jnp.where(hit, 1.0, 0.0)
    tile[...] = jnp.zeros_like(tile)
    tile[0:EXP, 0:TOK] = dense
    tile[EXP : 2 * EXP, 0:TOK] = named
    table = jnp.transpose(tile[...])[0:ROWS, :]
    earlier = jnp.where(
        lax.broadcasted_iota(I32, (ROWS, ROWS), 1) < lax.broadcasted_iota(I32, (ROWS, ROWS), 0), 1.0, 0.0
    ).astype(BF)
    lane = lax.broadcasted_iota(I32, (ROWS, 128), 1)
    slot = dot(earlier, table.astype(BF))
    slot = jnp.where(table > 0.5, slot, -1.0)
    gd[ep] = jnp.where((lane >= EXP) & (lane < 2 * EXP), slot, table).astype(BF)

    pl.semaphore_wait(barrier, EXP - 1 + 3)

    streams = (("x", 1), ("x", -1), ("y", 1), ("y", -1))

    def block_of(q, da, db):
        first, sign = streams[q]
        a, b = (x, y) if first == "x" else (y, x)
        a = lax.rem(a - sign * da + SIDE, SIDE)
        b = lax.rem(b - sign * db + SIDE, SIDE)
        return a * SIDE + b if first == "x" else b * SIDE + a

    def piece(q, da, db):
        return tok.at[block_of(q, da, db), pl.ds(q * 16, 16), :]

    def line_dev(q, phase):
        first, sign = streams[q]
        along_x = (first == "x") == (phase == 1)
        nx = lax.rem(x + sign + SIDE, SIDE) if along_x else x
        ny = y if along_x else lax.rem(y + sign + SIDE, SIDE)
        return {"ed": ed, "ep": nx * SIDE + ny}

    def xy_send1(q, j):
        ref = piece(q, j, 0)
        send(ref, ref, xy_s.at[q, j], xy_r.at[q, j], line_dev(q, 1))

    def xy_send2(q, j, i):
        m = 3 + 4 * j + i
        ref = piece(q, i, j)
        send(ref, ref, xy_s.at[q, m], xy_r.at[q, m], line_dev(q, 2))

    def xy_step(n):
        for q in range(4):
            if n < 3:
                arrived(piece(q, n + 1, 0), xy_r.at[q, n], xy_s.at[q, n])
                if n < 2:
                    xy_send1(q, n + 1)
                xy_send2(q, 0, n + 1)
            else:
                j, i = (n - 3) // 4, (n - 3) % 4
                arrived(piece(q, i, j + 1), xy_r.at[q, n], xy_s.at[q, n])
                if j < 2:
                    xy_send2(q, j + 1, i)

    def wpiece(d, k, core):
        zo = lax.rem(z - k + NZ, NZ) if d == 0 else lax.rem(z + k, NZ)
        return wts.at[zo * 2 + core, pl.ds(d * 128, 128), :]

    def w_pass(k):
        for d in range(2):
            ref = wpiece(d, k, c)
            if k > 0:
                arrived(ref, zw_r.at[d, k - 1], zw_s.at[d, k - 1])
            if k < NZ - 1:
                send(ref, ref, zw_s.at[d, k], zw_r.at[d, k], zdev(1 if d == 0 else -1))
            send(ref, ref, sw_s.at[d, k], sw_r.at[d, k], sibling)

    def gd_send(o, carry):
        send(gd.at[ep], gd.at[ep], gd_s.at[o], gd_r.at[o], {"ed": ed, "ep": peer(o)})
        return carry

    lax.fori_loop(1, EXP, gd_send, 0)
    for q in range(4):
        xy_send1(q, 0)
    w_pass(0)
    for q in range(4):
        xy_send2(q, 0, 0)

    def gd_wait(o, carry):
        arrived(gd.at[peer(EXP - o)], gd_r.at[o], gd_s.at[o])
        return carry

    lax.fori_loop(1, EXP, gd_wait, 0)

    def choose(r):
        rows = pl.ds(r * 256, 256)
        mine = gd[4 * r : 4 * r + 4].reshape(256, 128).astype(F32)
        lanes = lax.broadcasted_iota(I32, (256, 128), 1)
        gate = jnp.sum(jnp.where(lanes == ep, mine, 0.0), axis=1, keepdims=True)
        place = jnp.sum(jnp.where(lanes == EXP + ep, mine, 0.0), axis=1, keepdims=True)
        source = (lax.broadcasted_iota(I32, (256, 1), 0) // ROWS + 4 * r).astype(F32)
        target = jnp.where(place >= 0.0, place * EXP + source, -1.0)
        gatec[rows, :] = jnp.broadcast_to(gate, (256, 128))
        turned = jnp.transpose(jnp.where(lanes == 0, target, jnp.where(lanes == 1, gate, 0.0)))
        slots_down = lax.broadcasted_iota(I32, (SLOTS, 256), 0).astype(F32)
        same = slots_down == turned[0:1, :]
        sel_t[:, rows] = jnp.where(same, 1.0, 0.0).astype(BF)
        gated = jnp.where(same, turned[1:2, :], 0.0).astype(BF)
        for f in range(3):
            cols = pl.ds(f * 512, 512)
            hg_t[cols, rows] = lax.dot_general(
                hid_ref[:, cols], gated, (((0,), (0,)), ((), ())), preferred_element_type=F32
            ).astype(BF)
        slots_across = lax.broadcasted_iota(I32, (256, SLOTS), 1).astype(F32)
        picked = jnp.where(slots_across == target, 1.0, 0.0).astype(BF)
        h_tok[rows, :] = dot(picked, hid_ref[...]).astype(BF)

    def p_compute(k, settled):
        place = lax.rem(k, 2)
        for d in range(2):
            zo = lax.rem(z - 1 - k + 2 * NZ, NZ) if d == 0 else lax.rem(z + 1 + k, NZ)
            left = hg_t[d * HALF : (d + 1) * HALF, :]

            def side(core):
                cols = pl.ds(pl.multiple_of((zo * 2 + core) * OWN, OWN), OWN)
                return tok[:, :, cols].reshape(ALL, OWN)

            if settled:
                sent(stage.at[d, place], ps_s.at[d, k - 2], ps_r.at[d, k - 2])
            stage[d, place] = dot(left, side(1 - c)).astype(BF)
            send(stage.at[d, place], psib.at[d, k], ps_s.at[d, k], ps_r.at[d, k], sibling)
            pown[d, place] = dot(left, side(c))

    def rs_step(k, first):
        place = lax.rem(k, 2)
        for d in range(2):
            arrived(psib.at[d, k], ps_r.at[d, k], ps_s.at[d, k])
            total = pown[d, place] + psib[d, k].astype(F32)
            if not first:
                arrived(rsb.at[d, k], rs_r.at[d, k - 1], rs_s.at[d, k - 1])
                total = total + rsb[d, k].astype(F32)
            rsb[d, k] = total.astype(BF)
            send(rsb.at[d, k], rsb.at[d, k + 1], rs_s.at[d, k], rs_r.at[d, k], zdev(1 if d == 0 else -1))

    def up_part(n):
        cols = pl.ds(pl.multiple_of(n * COL, COL), COL)
        acc[...] = jnp.zeros_like(acc)

        def deep(kk, carry):
            t = tok[:, :, pl.ds(pl.multiple_of(kk * 512, 512), 512)].reshape(ALL, 512)
            w = wts[pl.ds(kk * 2, 2), :, cols].reshape(512, COL)
            acc[...] += dot(t, w)
            return carry

        lax.fori_loop(0, WIDTH // 512, deep, 0)

        def finish(r, carry):
            rows = pl.ds(pl.multiple_of(r * 256, 256), 256)
            up = acc[rows, :]
            prod = up * h_tok[rows, cols].astype(F32)
            prob[rows, :] += prod[:, 0:128] + prod[:, 128:256]
            gate = gatec[rows, :]
            gmul[rows, :] = (jnp.concatenate([gate, gate], axis=1) * up).astype(BF)
            return carry

        lax.fori_loop(0, ALL // 256, finish, 0)
        gh_ref[:, cols] = dot(sel_t[...], gmul[...]).astype(BF)

    prob[...] = jnp.zeros_like(prob)
    xy_step(0)
    choose(0)
    xy_step(1)
    w_pass(1)
    choose(1)
    xy_step(2)
    xy_step(3)
    choose(2)
    xy_step(4)
    w_pass(2)
    choose(3)
    xy_step(5)
    xy_step(6)
    xy_step(7)
    w_pass(3)
    xy_step(8)
    xy_step(9)
    xy_step(10)
    w_pass(4)
    xy_step(11)
    xy_step(12)
    xy_step(13)
    w_pass(5)
    xy_step(14)
    p_compute(0, False)
    w_pass(6)
    p_compute(1, False)
    rs_step(0, True)
    w_pass(7)
    for k in range(NZ):
        for d in range(2):
            arrived(wpiece(d, k, 1 - c), sw_r.at[d, k], sw_s.at[d, k])

    def main(k, carry):
        p_compute(k + 1, True)
        up_part(k - 1)
        rs_step(k, False)
        return carry

    lax.fori_loop(1, NZ - 1, main, 0)

    for r in range(4):
        rows = pl.ds(r * 256, 256)
        prob[rows, :] = jnp.broadcast_to(jnp.sum(prob[rows, :], axis=1, keepdims=True), (256, 128))

    def prob_at(s):
        return prob.at[pl.ds(pl.multiple_of(s * ROWS, ROWS), ROWS), :]

    def pr_send(o, carry):
        send(prob_at(peer(o)), probr.at[ep], pr_s.at[o], pr_r.at[o], {"ed": ed, "ep": peer(o)})
        return carry

    lax.fori_loop(1, EXP, pr_send, 0)
    probr[ep] = prob[pl.ds(pl.multiple_of(ep * ROWS, ROWS), ROWS), :]

    for d in range(2):
        arrived(psib.at[d, NZ - 1], ps_r.at[d, NZ - 1], ps_s.at[d, NZ - 1])
        arrived(rsb.at[d, NZ - 1], rs_r.at[d, NZ - 2], rs_s.at[d, NZ - 2])
        total = pown[d, (NZ - 1) % 2] + psib[d, NZ - 1].astype(F32) + rsb[d, NZ - 1].astype(F32)
        grad_ref[:, d * HALF : (d + 1) * HALF] = jnp.transpose(total)

    def pr_wait(o, carry):
        arrived(probr.at[peer(EXP - o)], pr_r.at[o], pr_s.at[o])
        return carry

    lax.fori_loop(1, EXP, pr_wait, 0)
    lanes = lax.broadcasted_iota(I32, (ROWS, 128), 1)
    spread = jnp.zeros((ROWS, 128), F32)
    for e in range(EXP):
        spread = jnp.where(lanes == e, probr[e], spread)
    tile[0:ROWS, :] = spread
    turned = jnp.transpose(tile[...])
    picked = jnp.zeros((routes_ref.shape[0], TOK), F32)
    for e in range(EXP):
        picked = picked + jnp.where(routes_ref[...] == e, turned[e : e + 1, 0:TOK], 0.0)
    gg_ref[...] = picked

    for q in range(4):
        for n in range(15):
            da, db = (n, 0) if n < 3 else ((n - 3) % 4, (n - 3) // 4)
            sent(piece(q, da, db), xy_s.at[q, n], xy_r.at[q, n])
    for d in range(2):
        for k in range(NZ):
            ref = wpiece(d, k, c)
            if k < NZ - 1:
                sent(ref, zw_s.at[d, k], zw_r.at[d, k])
                sent(rsb.at[d, k], rs_s.at[d, k], rs_r.at[d, k])
            sent(ref, sw_s.at[d, k], sw_r.at[d, k])
            if k >= NZ - 2:
                sent(stage.at[d, k % 2], ps_s.at[d, k], ps_r.at[d, k])

    def last(o, carry):
        sent(gd.at[ep], gd_s.at[o], gd_r.at[o])
        sent(prob_at(peer(o)), pr_s.at[o], pr_r.at[o])
        return carry

    lax.fori_loop(1, EXP, last, 0)


def local(grad_out, routes, gates, hidden, master, moment_one, moment_two):
    saved = jnp.transpose(hidden, (0, 2, 3, 1, 4)).reshape(SLOTS, HID)
    own = master.reshape(OWN, HID)
    vmem = pl.BlockSpec(memory_space=pltpu.VMEM)
    dma = pltpu.SemaphoreType.DMA
    gh, gradient, gg = pl.pallas_call(
        body,
        out_shape=(
            jax.ShapeDtypeStruct((SLOTS, HID), BF),
            jax.ShapeDtypeStruct((OWN, HID), F32),
            jax.ShapeDtypeStruct((routes.shape[1], TOK), F32),
        ),
        in_specs=[vmem] * 5,
        out_specs=(vmem,) * 3,
        scratch_shapes=[
            pltpu.VMEM((EXP, ROWS, WIDTH), BF),
            pltpu.VMEM((EXP, OWN, HID), BF),
            pltpu.VMEM((EXP, ROWS, 128), BF),
            pltpu.VMEM((128, 128), F32),
            pltpu.VMEM((ALL, 128), F32),
            pltpu.VMEM((SLOTS, ALL), BF),
            pltpu.VMEM((ALL, HID), BF),
            pltpu.VMEM((HID, ALL), BF),
            pltpu.VMEM((ALL, COL), F32),
            pltpu.VMEM((ALL, COL), BF),
            pltpu.VMEM((2, 2, HALF, OWN), F32),
            pltpu.VMEM((2, 2, HALF, OWN), BF),
            pltpu.VMEM((2, NZ, HALF, OWN), BF),
            pltpu.VMEM((2, NZ, HALF, OWN), BF),
            pltpu.VMEM((ALL, 128), F32),
            pltpu.VMEM((EXP, ROWS, 128), F32),
            dma((4, 15)), dma((4, 15)),
            dma((2, NZ - 1)), dma((2, NZ - 1)),
            dma((2, NZ)), dma((2, NZ)),
            dma((EXP,)), dma((EXP,)),
            dma((2, NZ)), dma((2, NZ)),
            dma((2, NZ - 1)), dma((2, NZ - 1)),
            dma((EXP,)), dma((EXP,)),
        ],
        compiler_params=pltpu.CompilerParams(
            collective_id=0, has_side_effects=True, vmem_limit_bytes=62 * 1024 * 1024
        ),
        cost_estimate=pl.CostEstimate(flops=25_000_000_000, bytes_accessed=8_000_000, transcendentals=0),
        name="expert_backward",
    )(grad_out, routes.T, gates.T, saved, own)

    gradient = gradient.reshape(master.shape)
    new_moment_one = beta_first * moment_one + (1.0 - beta_first) * gradient
    new_moment_two = beta_second * moment_two + (1.0 - beta_second) * gradient * gradient
    first_bias = 1.0 - beta_first**20
    second_bias = 1.0 - beta_second**20
    update = new_moment_one / first_bias / (jnp.sqrt(new_moment_two / second_bias) + adam_eps)
    new_master = master - learn_rate * update
    grad_hidden = jnp.transpose(gh.reshape(1, 1, CAP, EXP, HID), (0, 3, 1, 2, 4))
    return (gg.T, grad_hidden, new_master, new_moment_one, new_moment_two)


def solution(mesh):
    in_specs = (
        P(("ed", "ep"), None),
        P(("ed", "ep"), None),
        P(("ed", "ep"), None),
        P("ed", None, "ep", None, None),
        P("ep", "ed", None),
        P("ep", "ed", None),
        P("ep", "ed", None),
    )
    out_specs = (
        P(("ed", "ep"), None),
        P("ed", None, "ep", None, None),
        P("ep", "ed", None),
        P("ep", "ed", None),
        P("ep", "ed", None),
    )
    return jax.shard_map(local, mesh=mesh, in_specs=in_specs, out_specs=out_specs, check_vma=False)
```

time: 345 us -> 171 us (0.50)
  waiting for transfers between devices: 234 us -> 0 us
  Pallas kernels: 0 us -> 160 us
  matrix products: 31 us -> 0 us
  local copies, waits for them, and re-layouts: 28.7 us -> 1.8 us
  starting transfers between devices: 21.1 us -> 0 us
  between operations: 14.2 us -> 0.67 us
  other arithmetic: 15.8 us -> 5.4 us
    pallas_call x0 -> x1, Pallas kernels: none -> 160 us  [local(): pl.pallas_call(body, out_shape=(jax.ShapeDtypeStruct((SLOTS, HID), BF), j...]
    reduce_scatter x1 -> x0, waiting for transfers between devices: 85.1 us -> none  [local(): lax.psum_scatter(lax.dot_general(weighted, saved_rows, (((0,), (0,)), (()...]
    all_to_all x3 -> x0, waiting for transfers between devices: 77.2 us -> none  [the longest x1 74.3 us: local(): lax.all_to_all(send_rows.reshape(experts, 1, capacity, model_width), 'ep'...]
    all_gather x1 -> x0, waiting for transfers between devices: 71.9 us -> none  [local(): block = lax.all_gather(weights, 'ed', axis=1, tiled=True)[0]]
    dot_general x3 -> x0, matrix products: 31 us -> none  [the longest x1 14.8 us: local(): lax.dot_general(weighted, saved_rows, (((0,), (0,)), ((), ())), preferred...]
    all_to_all x3 -> x0, starting transfers between devices: 20.8 us -> none  [the longest x1 7.58 us: local(): lax.all_to_all(send_gates.reshape(experts, 1, capacity), 'ep', split_axis...]
    reshape x6 -> x0, local copies, waits for them, and re-layouts: 13.4 us -> none  [the longest x1 4.72 us: local(): grad_rows = rows_in.reshape(row_count, model_width)]
    convert_element_type x3 -> x0, other arithmetic: 6.87 us -> none  [the longest x1 6.83 us: local(): weighted = (gate_rows * grad_rows.astype(jnp.float32)).astype(jnp.bfloat16)]
  transfers between devices with their start and end apart: 5 -> 0, of which waited for: 4 -> 0; matrix products, arithmetic and copies ran while one was open for 6% -> 0% of each run, Pallas kernels for 0% -> 0%
where the time goes in v1:
time: 171 us; the launch traced here: 168 us
  Pallas kernels  160 us (94%)
  other arithmetic  5.4 us (3%)
  local copies, waits for them, and re-layouts  1.8 us (1%)
    pallas_call x1, Pallas kernels, local(): pl.pallas_call(body, out_shape=(jax.ShapeDtypeStruct((SLOTS, HID), BF), j...  160 us
    sub x1, other arithmetic, local(): new_master = master - learn_rate * update  5.4 us

profile of v1, /device:TPU:1, one launch (start us, length us, event | category | flops | bytes accessed | tf_op | source)
XLA Modules:
  0.0 167.7 jit_solution(11646167750786874560)
XLA Ops:
  0.6 0.0 copy-start.1
  0.6 159.9 %expert_backward.1 = (bf16[560,1536]{1,0:T(8,128)(2,1)}, f32[256,1536]{1,0:T(8,128)}, f32[8,56]{1,0:T(8,128)}) custom-call(bf16[56,4096]{1,0:T(8,128)(2,1)} %go_ref.1, s32[8,56]{1,0:T(8,128)} %bitcast.22, bf16[8,56]{1,0:T(8,128)(2,1)} %bitcast.23, bf16[560,1536]{1,0:T(8,128)(2,1)} %bitcast.21, f32[256,1536]{1,0:T(8,128)} %bitcast.19), custom_call_target="tpu_custom_call" | custom-call | flops 24999999488 | bytes 8000000 | tf_op jit(solution)/shard_map/expert_backward/pallas_call | solution.py:361
  160.5 0.0 copy-done.1
  160.5 0.0 copy-start.2
  160.5 0.0 copy-start
  160.6 5.4 %multiply_subtract_fusion = (f32[1,256,1536]{2,1,0:T(8,128)}, f32[1,256,1536]{2,1,0:T(8,128)}, f32[1,256,1536]{2,1,0:T(8,128)}) fusion(f32[1,256,1536]{2,1,0:T(8,128)S(1)} %copy-done.1, f32[256,1536]{1,0:T(8,128)} %get-tuple-element.10, f32[1,256,1536]{2,1,0:T(8,128)} %param.12, f32[1,256,1536]{2,1,0:T(8,128)} %param.13), kind=kLoop, calls=%fused_computation.4 | loop fusion | flops 5111808 | bytes 11010048 | tf_op jit(solution)/shard_map/sub | solution.py:408
  165.9 0.0 copy-done.2
  166.0 0.6 copy.14
  166.5 0.0 copy-done
  166.5 1.2 copy.15
Async XLA Ops:
  0.6 159.9 %copy-start.1 = (f32[1,256,1536]{2,1,0:T(8,128)S(1)}, f32[1,256,1536]{2,1,0:T(8,128)}, u32[]{:S(2)}) copy-start(f32[1,256,1536]{2,1,0:T(8,128)} %param.11) | copy-start | bytes 4718596
  160.5 5.4 %copy-start.2 = (f32[8,56]{1,0:T(8,128)S(1)}, f32[8,56]{1,0:T(8,128)}, u32[]{:S(2)}) copy-start(f32[8,56]{1,0:T(8,128)} %get-tuple-element.8) | copy-start | bytes 5380
  160.5 6.0 %copy-start = (bf16[560,1536]{1,0:T(8,128)(2,1)S(1)}, bf16[560,1536]{1,0:T(8,128)(2,1)}, u32[]{:S(2)}) copy-start(bf16[560,1536]{1,0:T(8,128)(2,1)} %get-tuple-element.9) | copy-start | bytes 5160964

commit v2 on v1

v2 whole, which is shorter than its diff:
```python
import jax
import jax.numpy as jnp
from jax import lax
from jax.experimental import pallas as pl
from jax.experimental.pallas import tpu as pltpu
from jax.sharding import PartitionSpec as P

beta_first = 0.9
beta_second = 0.95
learn_rate = 0.01
adam_eps = 1e-08

MESH = pl.DeviceIdType.MESH
BF = jnp.bfloat16
F32 = jnp.float32
I32 = jnp.int32

NZ = 8
SIDE = 4
EXP = 16
TOK = 56
ROWS = 64
ALL = EXP * ROWS
WIDTH = 4096
HID = 1536
HALF = HID // 2
CAP = 35
SLOTS = CAP * EXP
OWN = 256
COL = 256
LIMIT = 58
XY_PACE = 3.2
NSUB = 2
WSUB = OWN // NSUB
RSUB = HALF // NSUB


def dot(a, b):
    return jnp.dot(a, b, preferred_element_type=F32)


def body(
    go_ref, routes_ref, gates_ref, hid_hbm, master_hbm,
    gh_hbm, grad_hbm, gg_ref,
    tok, wts, gd, tile, gatec, sel_t, h_tok, hg_t, u, gmul, hid_ref, gh_part, pown, stage, psib, rsb, prob, probr,
    xy_s, xy_r, zw_s, zw_r, sw_s, sw_r, gd_s, gd_r, ps_s, ps_r, rs_s, rs_r, pr_s, pr_r, in_sem, gh_sem, grad_sem,
):
    ed = lax.axis_index("ed")
    ep = lax.axis_index("ep")
    z, c = ed // 2, ed % 2
    x, y = ep // SIDE, ep % SIDE

    def zdev(k):
        return {"ed": lax.rem(z + k + NZ, NZ) * 2 + c, "ep": ep}

    sibling = {"ed": z * 2 + 1 - c, "ep": ep}

    def peer(o):
        return lax.rem(ep + o, EXP)

    def send(src, dst, ssem, rsem, dev):
        copy = pltpu.make_async_remote_copy(
            src_ref=src, dst_ref=dst, send_sem=ssem, recv_sem=rsem,
            device_id=dev, device_id_type=MESH,
        )
        copy.start()

    def arrived(ref, rsem, ssem):
        pltpu.make_async_remote_copy(
            src_ref=ref, dst_ref=ref, send_sem=ssem, recv_sem=rsem,
            device_id=sibling, device_id_type=MESH,
        ).wait_recv()

    def sent(ref, ssem, rsem):
        pltpu.make_async_remote_copy(
            src_ref=ref, dst_ref=ref, send_sem=ssem, recv_sem=rsem,
            device_id=sibling, device_id_type=MESH,
        ).wait_send()

    load_master = pltpu.make_async_copy(master_hbm, u.at[pl.ds(0, OWN), :], in_sem.at[0])
    load_master.start()
    load_hid = pltpu.make_async_copy(hid_hbm, hid_ref, in_sem.at[1])
    load_hid.start()

    barrier = pltpu.get_barrier_semaphore()

    def greet(o, carry):
        pl.semaphore_signal(barrier, inc=1, device_id={"ed": ed, "ep": peer(o)}, device_id_type=MESH)
        return carry

    lax.fori_loop(1, EXP, greet, 0)
    for dev in (zdev(1), zdev(-1), sibling):
        pl.semaphore_signal(barrier, inc=1, device_id=dev, device_id_type=MESH)

    load_master.wait()
    wts[ed] = u[0:OWN, :].astype(BF)
    pl.semaphore_wait(barrier, EXP - 1 + 3)

    def wpiece(d, k, core, part):
        zo = lax.rem(z - k + NZ, NZ) if d == 0 else lax.rem(z + k, NZ)
        return wts.at[zo * 2 + core, pl.ds(part * WSUB, WSUB), pl.ds(d * HALF, HALF)]

    def w_pass(k, part):
        for d in range(2):
            ref = wpiece(d, k, c, part)
            if k > 0:
                arrived(ref, zw_r.at[d, k - 1, part], zw_s.at[d, k - 1, part])
            if k < NZ - 1:
                send(ref, ref, zw_s.at[d, k, part], zw_r.at[d, k, part], zdev(1 if d == 0 else -1))
        for d in range(2):
            ref = wpiece(d, k, c, part)
            send(ref, ref, sw_s.at[d, k, part], sw_r.at[d, k, part], sibling)

    w_pass(0, 0)

    for q in range(4):
        cols = pl.ds(q * 1024, 1024)
        wide = go_ref[:, cols].astype(F32)
        tok[ep, :, cols] = jnp.concatenate([wide, jnp.zeros((ROWS - TOK, 1024), F32)], axis=0).astype(BF)

    streams = (("x", 1), ("x", -1), ("y", 1), ("y", -1))

    def block_of(q, da, db):
        first, sign = streams[q]
        a, b = (x, y) if first == "x" else (y, x)
        a = lax.rem(a - sign * da + SIDE, SIDE)
        b = lax.rem(b - sign * db + SIDE, SIDE)
        return a * SIDE + b if first == "x" else b * SIDE + a

    def piece(q, da, db):
        return tok.at[block_of(q, da, db), pl.ds(q * 16, 16), :]

    def line_dev(q, phase):
        first, sign = streams[q]
        along_x = (first == "x") == (phase == 1)
        nx = lax.rem(x + sign + SIDE, SIDE) if along_x else x
        ny = y if along_x else lax.rem(y + sign + SIDE, SIDE)
        return {"ed": ed, "ep": nx * SIDE + ny}

    def xy_send1(q, j):
        ref = piece(q, j, 0)
        send(ref, ref, xy_s.at[q, j], xy_r.at[q, j], line_dev(q, 1))

    def xy_send2(q, j, i):
        m = 3 + 4 * j + i
        ref = piece(q, i, j)
        send(ref, ref, xy_s.at[q, m], xy_r.at[q, m], line_dev(q, 2))

    def xy_step(n):
        for q in range(4):
            if n < 3:
                arrived(piece(q, n + 1, 0), xy_r.at[q, n], xy_s.at[q, n])
                if n < 2:
                    xy_send1(q, n + 1)
                xy_send2(q, 0, n + 1)
            else:
                j, i = (n - 3) // 4, (n - 3) % 4
                arrived(piece(q, i, j + 1), xy_r.at[q, n], xy_s.at[q, n])
                if j < 2:
                    xy_send2(q, j + 1, i)

    for q in range(4):
        xy_send1(q, 0)
    for q in range(4):
        xy_send2(q, 0, 0)

    w_pass(0, 1)

    expert_row = lax.broadcasted_iota(I32, (EXP, TOK), 0)
    dense = jnp.zeros((EXP, TOK), F32)
    named = jnp.zeros((EXP, TOK), F32)
    for k in range(routes_ref.shape[0]):
        hit = routes_ref[k : k + 1, :] == expert_row
        dense = dense + jnp.where(hit, gates_ref[k : k + 1, :].astype(F32), 0.0)
        named = named + jnp.where(hit, 1.0, 0.0)
    tile[...] = jnp.zeros_like(tile)
    tile[0:EXP, 0:TOK] = dense
    tile[EXP : 2 * EXP, 0:TOK] = named
    table = jnp.transpose(tile[...])[0:ROWS, :]
    earlier = jnp.where(
        lax.broadcasted_iota(I32, (ROWS, ROWS), 1) < lax.broadcasted_iota(I32, (ROWS, ROWS), 0), 1.0, 0.0
    ).astype(BF)
    lane = lax.broadcasted_iota(I32, (ROWS, 128), 1)
    slot = dot(earlier, table.astype(BF))
    slot = jnp.where(table > 0.5, slot, -1.0)
    gd[ep] = jnp.where((lane >= EXP) & (lane < 2 * EXP), slot, table).astype(BF)


    def gd_send(o, carry):
        send(gd.at[ep], gd.at[ep], gd_s.at[o], gd_r.at[o], {"ed": ed, "ep": peer(o)})
        return carry

    lax.fori_loop(1, EXP, gd_send, 0)

    def gd_wait(o, carry):
        arrived(gd.at[peer(EXP - o)], gd_r.at[o], gd_s.at[o])
        return carry

    u[...] = jnp.zeros_like(u)
    prob[...] = jnp.zeros_like(prob)

    def choose(r):
        rows = pl.ds(r * 256, 256)
        mine = gd[4 * r : 4 * r + 4].reshape(256, 128).astype(F32)
        lanes = lax.broadcasted_iota(I32, (256, 128), 1)
        gate = jnp.sum(jnp.where(lanes == ep, mine, 0.0), axis=1, keepdims=True)
        place = jnp.sum(jnp.where(lanes == EXP + ep, mine, 0.0), axis=1, keepdims=True)
        source = (lax.broadcasted_iota(I32, (256, 1), 0) // ROWS + 4 * r).astype(F32)
        target = jnp.where(place >= 0.0, place * EXP + source, -1.0)
        gatec[rows, :] = jnp.broadcast_to(gate, (256, 128))
        turned = jnp.transpose(jnp.where(lanes == 0, target, jnp.where(lanes == 1, gate, 0.0)))
        slots_down = lax.broadcasted_iota(I32, (SLOTS, 256), 0).astype(F32)
        same = slots_down == turned[0:1, :]
        sel_t[:, rows] = jnp.where(same, 1.0, 0.0).astype(BF)
        gated = jnp.where(same, turned[1:2, :], 0.0).astype(BF)
        for f in range(3):
            cols = pl.ds(f * 512, 512)
            hg_t[cols, rows] = lax.dot_general(
                hid_ref[:, cols], gated, (((0,), (0,)), ((), ())), preferred_element_type=F32
            ).astype(BF)
        slots_across = lax.broadcasted_iota(I32, (256, SLOTS), 1).astype(F32)
        picked = jnp.where(slots_across == target, 1.0, 0.0).astype(BF)
        for f in range(3):
            cols = pl.ds(f * 512, 512)
            h_tok[rows, cols] = dot(picked, hid_ref[:, cols]).astype(BF)

    def p_compute(k, settled):
        place = lax.rem(k, 2)
        for d in range(2):
            zo = lax.rem(z - 1 - k + 2 * NZ, NZ) if d == 0 else lax.rem(z + 1 + k, NZ)

            def side(core):
                cols = pl.ds(pl.multiple_of((zo * 2 + core) * OWN, OWN), OWN)
                return tok[:, :, cols].reshape(ALL, OWN)

            if settled:
                sent(stage.at[d, place], ps_s.at[d, k - 2], ps_r.at[d, k - 2])
            for part in range(NSUB):
                rows = pl.ds(part * RSUB, RSUB)
                stage[d, place, rows, :] = dot(hg_t[pl.ds(d * HALF + part * RSUB, RSUB), :], side(1 - c)).astype(BF)
            send(stage.at[d, place], psib.at[d, k], ps_s.at[d, k], ps_r.at[d, k], sibling)
            for part in range(NSUB):
                rows = pl.ds(part * RSUB, RSUB)
                pown[d, place, rows, :] = dot(hg_t[pl.ds(d * HALF + part * RSUB, RSUB), :], side(c)).astype(BF)

    def rs_part(k, part, first):
        place = lax.rem(k, 2)
        rows = pl.ds(part * RSUB, RSUB)
        for d in range(2):
            if part == 0:
                arrived(psib.at[d, k], ps_r.at[d, k], ps_s.at[d, k])
            total = pown[d, place, rows, :].astype(F32) + psib[d, k, rows, :].astype(F32)
            here = rsb.at[d, k, rows, :]
            if not first:
                arrived(here, rs_r.at[d, k - 1, part], rs_s.at[d, k - 1, part])
                total = total + here[...].astype(F32)
            here[...] = total.astype(BF)
            send(
                here, rsb.at[d, k + 1, rows, :],
                rs_s.at[d, k, part], rs_r.at[d, k, part], zdev(1 if d == 0 else -1),
            )

    def up_step(k, carry):
        for d in range(2):
            zo = lax.rem(z - k + NZ, NZ) if d == 0 else lax.rem(z + k, NZ)
            deep = pl.ds(pl.multiple_of(zo * 512, 512), 512)
            for f in range(HALF // COL):
                cols = pl.ds(d * HALF + f * COL, COL)
                t = tok[:, :, deep].reshape(ALL, 512)
                u[:, cols] += dot(t, wts[pl.ds(zo * 2, 2), :, cols].reshape(512, COL))
        return carry

    def gh_copy(n):
        return pltpu.make_async_copy(
            gh_part.at[n % 2], gh_hbm.at[:, pl.ds(n * COL, COL)], gh_sem.at[n % 2]
        )

    def finish(n):
        cols = pl.ds(n * COL, COL)

        def some(r, carry):
            rows = pl.ds(pl.multiple_of(r * 256, 256), 256)
            up = u[rows, cols]
            prod = up * h_tok[rows, cols].astype(F32)
            prob[rows, :] += prod[:, 0:128] + prod[:, 128:256]
            gate = gatec[rows, :]
            gmul[rows, :] = (jnp.concatenate([gate, gate], axis=1) * up).astype(BF)
            return carry

        lax.fori_loop(0, ALL // 256, some, 0)
        if n >= 2:
            gh_copy(n - 2).wait()
        gh_part[n % 2] = dot(sel_t[...], gmul[...]).astype(BF)
        gh_copy(n).start()

    def sw_wait(k):
        for d in range(2):
            for part in range(NSUB):
                arrived(wpiece(d, k, 1 - c, part), sw_r.at[d, k, part], sw_s.at[d, k, part])

    due = [(XY_PACE * (n + 1), 0, n) for n in range(15)]
    due = due + [(8.0 / NSUB * (NSUB * k + part + 1) - 8.0, 1, k, part) for k in range(1, NZ) for part in range(NSUB)]
    selected, moved, seen = 0, False, 0
    after = 0
    for event in sorted(due):
        if event[1] == 0:
            xy_step(event[2])
            if event[2] == 14:
                p_compute(0, False)
                moved = True
        else:
            w_pass(event[2], event[3])
            if moved:
                after = after + 1
                if after == 1:
                    p_compute(1, False)
                if after == 2:
                    rs_part(0, 0, True)
                    sw_wait(0)
                    up_step(0, 0)
                    rs_part(0, 1, True)
                if after == 3:
                    sw_wait(1)
                    up_step(1, 0)
        seen = seen + 1
        if seen == 3:
            lax.fori_loop(1, EXP, gd_wait, 0)
            load_hid.wait()
        if seen >= 3 and selected < 4:
            choose(selected)
            selected = selected + 1
    for k in range(2, NZ):
        sw_wait(k)

    def early(k, carry):
        p_compute(k + 1, True)
        for part in range(NSUB):
            rs_part(k, part, False)
            up_step(NSUB * (k - 1) + part + 2, 0)
        return carry

    lax.fori_loop(1, 4, early, 0)
    for k in range(4, 6):
        p_compute(k + 1, True)
        for part in range(NSUB):
            rs_part(k, part, False)
            finish(3 * (k - 4) + part)
        finish(3 * (k - 4) + 2)

    for r in range(4):
        rows = pl.ds(r * 256, 256)
        prob[rows, :] = jnp.broadcast_to(jnp.sum(prob[rows, :], axis=1, keepdims=True), (256, 128))

    def prob_at(s):
        return prob.at[pl.ds(pl.multiple_of(s * ROWS, ROWS), ROWS), :]

    def pr_send(o, carry):
        send(prob_at(peer(o)), probr.at[ep], pr_s.at[o], pr_r.at[o], {"ed": ed, "ep": peer(o)})
        return carry

    lax.fori_loop(1, EXP, pr_send, 0)
    probr[ep] = prob[pl.ds(pl.multiple_of(ep * ROWS, ROWS), ROWS), :]

    p_compute(NZ - 1, True)
    for part in range(NSUB):
        rs_part(NZ - 2, part, False)

    for q in range(4):
        for n in range(15):
            da, db = (n, 0) if n < 3 else ((n - 3) % 4, (n - 3) // 4)
            sent(piece(q, da, db), xy_s.at[q, n], xy_r.at[q, n])
    for d in range(2):
        for k in range(NZ):
            for part in range(NSUB):
                ref = wpiece(d, k, c, part)
                if k < NZ - 1:
                    sent(ref, zw_s.at[d, k, part], zw_r.at[d, k, part])
                sent(ref, sw_s.at[d, k, part], sw_r.at[d, k, part])
                if k < NZ - 2:
                    here = rsb.at[d, k, pl.ds(part * RSUB, RSUB), :]
                    sent(here, rs_s.at[d, k, part], rs_r.at[d, k, part])

    def last(o, carry):
        sent(gd.at[ep], gd_s.at[o], gd_r.at[o])
        return carry

    lax.fori_loop(1, EXP, last, 0)
    gh_copy(4).wait()
    gh_copy(5).wait()

    def pr_wait(o, carry):
        arrived(probr.at[peer(EXP - o)], pr_r.at[o], pr_s.at[o])
        return carry

    lax.fori_loop(1, EXP, pr_wait, 0)
    lanes = lax.broadcasted_iota(I32, (ROWS, 128), 1)
    spread = jnp.zeros((ROWS, 128), F32)
    for e in range(EXP):
        spread = jnp.where(lanes == e, probr[e], spread)
    tile[0:ROWS, :] = spread
    turned = jnp.transpose(tile[...])
    picked = jnp.zeros((routes_ref.shape[0], TOK), F32)
    for e in range(EXP):
        picked = picked + jnp.where(routes_ref[...] == e, turned[e : e + 1, 0:TOK], 0.0)
    gg_ref[...] = picked

    def grad_copy(d, part):
        cols = pl.ds(d * HALF + part * RSUB, RSUB)
        return pltpu.make_async_copy(u.at[pl.ds(0, OWN), cols], grad_hbm.at[:, cols], grad_sem.at[d, part])

    for part in range(NSUB):
        rows = pl.ds(part * RSUB, RSUB)
        for d in range(2):
            if part == 0:
                arrived(psib.at[d, NZ - 1], ps_r.at[d, NZ - 1], ps_s.at[d, NZ - 1])
            total = pown[d, (NZ - 1) % 2, rows, :].astype(F32) + psib[d, NZ - 1, rows, :].astype(F32)
            here = rsb.at[d, NZ - 1, rows, :]
            arrived(here, rs_r.at[d, NZ - 2, part], rs_s.at[d, NZ - 2, part])
            total = total + here[...].astype(F32)
            u[0:OWN, d * HALF + part * RSUB : d * HALF + (part + 1) * RSUB] = jnp.transpose(total)
            grad_copy(d, part).start()

    for d in range(2):
        for part in range(NSUB):
            here = rsb.at[d, NZ - 2, pl.ds(part * RSUB, RSUB), :]
            sent(here, rs_s.at[d, NZ - 2, part], rs_r.at[d, NZ - 2, part])
        for k in range(NZ - 2, NZ):
            sent(stage.at[d, k % 2], ps_s.at[d, k], ps_r.at[d, k])

    def pr_last(o, carry):
        sent(prob_at(peer(o)), pr_s.at[o], pr_r.at[o])
        return carry

    lax.fori_loop(1, EXP, pr_last, 0)
    for d in range(2):
        for part in range(NSUB):
            grad_copy(d, part).wait()


def local(grad_out, routes, gates, hidden, master, moment_one, moment_two):
    saved = jnp.transpose(hidden, (0, 2, 3, 1, 4)).reshape(SLOTS, HID)
    own = master.reshape(OWN, HID)
    vmem = pl.BlockSpec(memory_space=pltpu.VMEM)
    dma = pltpu.SemaphoreType.DMA
    gh, gradient, gg = pl.pallas_call(
        body,
        out_shape=(
            jax.ShapeDtypeStruct((SLOTS, HID), BF),
            jax.ShapeDtypeStruct((OWN, HID), F32),
            jax.ShapeDtypeStruct((routes.shape[1], TOK), F32),
        ),
        in_specs=[vmem] * 3 + [pl.BlockSpec(memory_space=pl.ANY)] * 2,
        out_specs=(pl.BlockSpec(memory_space=pl.ANY),) * 2 + (vmem,),
        scratch_shapes=[
            pltpu.VMEM((EXP, ROWS, WIDTH), BF),
            pltpu.VMEM((EXP, OWN, HID), BF),
            pltpu.VMEM((EXP, ROWS, 128), BF),
            pltpu.VMEM((128, 128), F32),
            pltpu.VMEM((ALL, 128), F32),
            pltpu.VMEM((SLOTS, ALL), BF),
            pltpu.VMEM((ALL, HID), BF),
            pltpu.VMEM((HID, ALL), BF),
            pltpu.VMEM((ALL, HID), F32),
            pltpu.VMEM((ALL, COL), BF),
            pltpu.VMEM((SLOTS, HID), BF),
            pltpu.VMEM((2, SLOTS, COL), BF),
            pltpu.VMEM((2, 2, HALF, OWN), BF),
            pltpu.VMEM((2, 2, HALF, OWN), BF),
            pltpu.VMEM((2, NZ, HALF, OWN), BF),
            pltpu.VMEM((2, NZ, HALF, OWN), BF),
            pltpu.VMEM((ALL, 128), F32),
            pltpu.VMEM((EXP, ROWS, 128), F32),
            dma((4, 15)), dma((4, 15)),
            dma((2, NZ - 1, NSUB)), dma((2, NZ - 1, NSUB)),
            dma((2, NZ, NSUB)), dma((2, NZ, NSUB)),
            dma((EXP,)), dma((EXP,)),
            dma((2, NZ)), dma((2, NZ)),
            dma((2, NZ - 1, NSUB)), dma((2, NZ - 1, NSUB)),
            dma((EXP,)), dma((EXP,)),
            dma((2,)), dma((2,)), dma((2, NSUB)),
        ],
        compiler_params=pltpu.CompilerParams(
            collective_id=0, has_side_effects=True, vmem_limit_bytes=LIMIT * 1024 * 1024
        ),
        cost_estimate=pl.CostEstimate(flops=25_000_000_000, bytes_accessed=8_000_000, transcendentals=0),
        name="expert_backward",
    )(grad_out, routes.T, gates.T, saved, own)

    gradient = gradient.reshape(master.shape)
    new_moment_one = beta_first * moment_one + (1.0 - beta_first) * gradient
    new_moment_two = beta_second * moment_two + (1.0 - beta_second) * gradient * gradient
    first_bias = 1.0 - beta_first**20
    second_bias = 1.0 - beta_second**20
    update = new_moment_one / first_bias / (jnp.sqrt(new_moment_two / second_bias) + adam_eps)
    new_master = master - learn_rate * update
    grad_hidden = jnp.transpose(gh.reshape(1, 1, CAP, EXP, HID), (0, 3, 1, 2, 4))
    return (gg.T, grad_hidden, new_master, new_moment_one, new_moment_two)


def solution(mesh):
    in_specs = (
        P(("ed", "ep"), None),
        P(("ed", "ep"), None),
        P(("ed", "ep"), None),
        P("ed", None, "ep", None, None),
        P("ep", "ed", None),
        P("ep", "ed", None),
        P("ep", "ed", None),
    )
    out_specs = (
        P(("ed", "ep"), None),
        P("ed", None, "ep", None, None),
        P("ep", "ed", None),
        P("ep", "ed", None),
        P("ep", "ed", None),
    )
    return jax.shard_map(local, mesh=mesh, in_specs=in_specs, out_specs=out_specs, check_vma=False)
```

time: 171 us -> 149 us (0.87); the launches traced: 168 us -> 149 us
  Pallas kernels: 160 us -> 142 us
    pallas_call x1, Pallas kernels: 160 us -> 142 us  [local(): pl.pallas_call(body, out_shape=(jax.ShapeDtypeStruct((SLOTS, HID), BF), j...]
where the time goes in v2:
time: 149 us
  Pallas kernels  142 us (95%)
  other arithmetic  4.45 us (3%)
  local copies, waits for them, and re-layouts  1.8 us (1%)
    pallas_call x1, Pallas kernels, local(): pl.pallas_call(body, out_shape=(jax.ShapeDtypeStruct((SLOTS, HID), BF), j...  142 us
    sub x1, other arithmetic, local(): new_master = master - learn_rate * update  4.45 us

profile of v2, /device:TPU:1, one launch (start us, length us, event | category | flops | bytes accessed | tf_op | source)
XLA Modules:
  0.0 148.8 jit_solution(7478090898325538679)
XLA Ops:
  0.6 0.0 copy-start.1
  0.6 0.0 copy-start.2
  0.7 0.0 copy-start.3
  0.7 141.9 %expert_backward.1 = (bf16[560,1536]{1,0:T(8,128)(2,1)}, f32[256,1536]{1,0:T(8,128)}, f32[8,56]{1,0:T(8,128)}) custom-call(bf16[56,4096]{1,0:T(8,128)(2,1)} %go_ref.1, s32[8,56]{1,0:T(8,128)} %bitcast.22, bf16[8,56]{1,0:T(8,128)(2,1)} %bitcast.23, bf16[560,1536]{1,0:T(8,128)(2,1)} %bitcast.21, f32[256,1536]{1,0:T(8,128)} %bitcast.19), custom_call_target="tpu_custom_call" | custom-call | flops 24999999488 | bytes 8000000 | tf_op jit(solution)/shard_map/expert_backward/pallas_call | solution.py:445
  142.5 0.0 copy-done.1
  142.5 0.0 copy-done.2
  142.6 0.0 copy-done.3
  142.6 0.0 copy-start.4
  142.6 0.0 copy-start
  142.6 4.5 %multiply_subtract_fusion = (f32[1,256,1536]{2,1,0:T(8,128)}, f32[1,256,1536]{2,1,0:T(8,128)}, f32[1,256,1536]{2,1,0:T(8,128)}) fusion(f32[1,256,1536]{2,1,0:T(8,128)S(1)} %copy-done.1, f32[256,1536]{1,0:T(8,128)} %get-tuple-element.10, f32[1,256,1536]{2,1,0:T(8,128)S(1)} %copy-done.2, f32[1,256,1536]{2,1,0:T(8,128)S(1)} %copy-done.3), kind=kLoop, calls=%fused_computation.4 | loop fusion | flops 5111808 | bytes 11010048 | tf_op jit(solution)/shard_map/sub | solution.py:495
  147.0 0.0 copy-done.4
  147.0 0.6 copy.14
  147.6 0.0 copy-done
  147.6 1.2 copy.15
Async XLA Ops:
  0.6 141.9 %copy-start.1 = (f32[1,256,1536]{2,1,0:T(8,128)S(1)}, f32[1,256,1536]{2,1,0:T(8,128)}, u32[]{:S(2)}) copy-start(f32[1,256,1536]{2,1,0:T(8,128)} %param.11) | copy-start | bytes 4718596
  0.6 141.9 %copy-start.2 = (f32[1,256,1536]{2,1,0:T(8,128)S(1)}, f32[1,256,1536]{2,1,0:T(8,128)}, u32[]{:S(2)}) copy-start(f32[1,256,1536]{2,1,0:T(8,128)} %param.12) | copy-start | bytes 4718596
  0.7 141.9 %copy-start.3 = (f32[1,256,1536]{2,1,0:T(8,128)S(1)}, f32[1,256,1536]{2,1,0:T(8,128)}, u32[]{:S(2)}) copy-start(f32[1,256,1536]{2,1,0:T(8,128)} %param.13) | copy-start | bytes 4718596
  142.6 4.5 %copy-start.4 = (f32[8,56]{1,0:T(8,128)S(1)}, f32[8,56]{1,0:T(8,128)}, u32[]{:S(2)}) copy-start(f32[8,56]{1,0:T(8,128)} %get-tuple-element.8) | copy-start | bytes 5380
  142.6 5.1 %copy-start = (bf16[560,1536]{1,0:T(8,128)(2,1)S(1)}, bf16[560,1536]{1,0:T(8,128)(2,1)}, u32[]{:S(2)}) copy-start(bf16[560,1536]{1,0:T(8,128)(2,1)} %get-tuple-element.9) | copy-start | bytes 5160964
